TPU v7x, 32 devices: a whole 2x2x4 slice. The times are simulated.
32 devices in a mesh: layer: 2 (over x), row: 4 (over y, core), col: 4 (over z).
Axes of the slice: x: 2, y: 2, z: 4, core: 2. Of those that a mesh axis runs over, the one named last changes fastest.
Arguments:
- density: bfloat16 [3200, 3200], P('row', 'col'), may hold values from -2 to 2
- density_mask: int32 [32, 32], P('row', 'col'), may hold values 0 or 1
- square_mask: int32 [32, 32], P('row', 'col'), may hold values 0 or 1
- result_mask: int32 [32, 32], P('row', 'col'), may hold values 0 or 1
- block_perm: int32 [32], replicated, may hold values from 0 to 31, as said below
Outputs:
- purified: bfloat16 [3200, 3200], P('row', 'col')
Inputs may be any that keep to these rules, and one draw needn't show every extreme that they name: `block_perm`: A permutation of the 32 block indices. For any two aligned groups of 8 indices, exactly 2 indices of the first group are mapped into the second group.
All inputs are finite; a program needn't handle non-finite values. No bound on the sum of `density_mask` or of `square_mask` or of `result_mask` on one device may be relied on, other than what follows from the above.
Results may differ from a plain program's by a relative error of at most 0.0049.
Values may be sent and summed in bfloat16 or wider, within the bound.
A program may use at most 64 MiB of HBM per device.

v0:
```python
import jax
import jax.numpy as jnp
from jax import lax
from jax.sharding import PartitionSpec as P


def passed_along(array, axis, by):
    count = lax.axis_size(axis)
    return lax.ppermute(array, axis, [(i, (i + by) % count) for i in range(count)])


def apply_pattern(values, pattern):
    count = pattern.shape[0]
    width = values.shape[0] // count
    shaped = values.reshape(count, width, count, width)
    shaped = shaped * pattern[:, None, :, None].astype(values.dtype)
    return shaped.reshape(count * width, count * width)


def pieces_out(values, mapping, row_group, col_group, groups):
    tile_blocks = mapping.shape[0] // groups
    width = values.shape[0] // tile_blocks
    per_pair = tile_blocks // groups
    row_order = jnp.argsort(lax.dynamic_slice_in_dim(mapping, row_group * tile_blocks, tile_blocks))
    col_order = jnp.argsort(lax.dynamic_slice_in_dim(mapping, col_group * tile_blocks, tile_blocks))
    shaped = values.reshape(tile_blocks, width, tile_blocks, width)
    shaped = jnp.take(shaped, row_order, axis=0)
    shaped = jnp.take(shaped, col_order, axis=2)
    shaped = shaped.reshape(groups, per_pair, width, groups, per_pair, width)
    shaped = shaped.transpose(0, 3, 1, 2, 4, 5)
    return shaped.reshape(groups * groups, per_pair * width, per_pair * width)


def source_rows(mapping, group, tile_blocks, per_pair):
    source = lax.dynamic_slice_in_dim(mapping, group * tile_blocks, tile_blocks) // tile_blocks
    positions = jnp.arange(tile_blocks, dtype=jnp.int32)
    same_group = source[:, None] == source[None, :]
    earlier = positions[None, :] < positions[:, None]
    ranking = jnp.sum(jnp.logical_and(same_group, earlier).astype(jnp.int32), axis=1)
    return source * per_pair + ranking


def assemble(received, mapping, row_group, col_group, groups):
    tile_blocks = mapping.shape[0] // groups
    per_pair = tile_blocks // groups
    width = received.shape[1] // per_pair
    shaped = received.reshape(groups, groups, per_pair, width, per_pair, width)
    shaped = shaped.transpose(0, 2, 3, 1, 4, 5).reshape(tile_blocks, width, tile_blocks, width)
    shaped = jnp.take(shaped, source_rows(mapping, row_group, tile_blocks, per_pair), axis=0)
    shaped = jnp.take(shaped, source_rows(mapping, col_group, tile_blocks, per_pair), axis=2)
    return shaped.reshape(tile_blocks * width, tile_blocks * width)


def skew_cols(values, amount, groups):
    for bit_index in range(groups.bit_length() - 1):
        moved = passed_along(values, "col", -(1 << bit_index))
        values = jnp.where(amount // (1 << bit_index) % 2 == 1, moved, values)
    return values


def skew_square(values, amount, groups):
    for bit_index in range(groups.bit_length() - 1):
        moved = passed_along(values, "col", -(1 << bit_index))
        values = jnp.where(amount // (1 << bit_index) % 2 == 1, moved, values)
    return values


def skew_rows(values, amount, groups):
    for bit_index in range(groups.bit_length() - 1):
        moved = passed_along(values, "row", -(1 << bit_index))
        values = jnp.where(amount // (1 << bit_index) % 2 == 1, moved, values)
    return values


def square_pass(left, right, steps):
    total = jnp.zeros((left.shape[0], right.shape[1]), jnp.float32)
    stored = []
    for step_index in range(steps):
        stored.append(right)
        total = total + jnp.dot(left, right, preferred_element_type=jnp.float32)
        if step_index + 1 < steps:
            left = passed_along(left, "col", -1)
            right = passed_along(right, "row", -1)
    return (total, stored)


def cube_pass(left, right, steps):
    total = jnp.zeros((left.shape[0], right.shape[1]), jnp.float32)
    for step_index in range(steps):
        factor = right
        total = total + jnp.dot(left, factor, preferred_element_type=jnp.float32)
        if step_index + 1 < steps:
            left = passed_along(left, "col", -1)
            right = passed_along(right, "row", -1)
    return total


def per_device(density, density_mask, square_mask, result_mask, block_perm):
    groups = lax.axis_size("row")
    steps = groups // lax.axis_size("layer")
    row_id = lax.axis_index("row")
    col_id = lax.axis_index("col")
    offset = lax.axis_index("layer") * steps
    inverse = jnp.argsort(block_perm)
    masked = apply_pattern(density, density_mask)
    pieces = pieces_out(masked, block_perm, row_id, col_id, groups)
    received = lax.all_to_all(pieces, ("row", "col"), split_axis=0, concat_axis=0, tiled=True)
    grid_tile = assemble(received, inverse, row_id, col_id, groups)
    left = skew_cols(grid_tile, (row_id + offset) % groups, groups)
    right = skew_rows(grid_tile, (col_id + offset) % groups, groups)
    square_part, stored = square_pass(left, right, steps)
    square_full = lax.psum(square_part, "layer")
    square = apply_pattern(square_full, square_mask).astype(jnp.bfloat16)
    square_left = skew_square(square, (row_id + offset) % groups, groups)
    cube_part = cube_pass(square_left, right, steps)
    cube = lax.psum(cube_part, "layer")
    result = apply_pattern(3.0 * square.astype(jnp.float32) - 2.0 * cube, result_mask).astype(
        jnp.bfloat16
    )
    outgoing = pieces_out(result, inverse, row_id, col_id, groups)
    returned = lax.all_to_all(outgoing, ("row", "col"), split_axis=0, concat_axis=0, tiled=True)
    return assemble(returned, block_perm, row_id, col_id, groups)


def solution(mesh):
    in_specs = (P("row", "col"), P("row", "col"), P("row", "col"), P("row", "col"), P())
    out_specs = P("row", "col")
    return jax.shard_map(
        per_device, mesh=mesh, in_specs=in_specs, out_specs=out_specs, check_vma=False
    )
```

profile of v0, /device:TPU:0, one launch (start us, length us, event | category | flops | bytes accessed | tf_op | source)
XLA Modules:
  0.0 590.8 jit_solution(8836765360884828955)
XLA Ops:
  6.5 2.3 sort.78
  8.8 0.8 and_select_fusion
  9.6 1.0 sort.76
  10.6 1.0 sort.77
  11.6 3.4 reshape.66
  15.2 0.9 gather_fusion
  16.3 1.1 copy.21
  17.4 1.2 gather_fusion.1
  18.8 1.3 copy.34
  20.1 1.9 reshape.68
  22.0 7.4 %all-to-all-start = ((bf16[16,200,200]{2,1,0:T(8,128)(2,1)}), bf16[16,200,200]{2,1,0:T(8,128)(2,1)S(1)}, u32[]{:S(2)}, u32[]{:S(2)}) async-start(bf16[16,200,200]{2,1,0:T(8,128)(2,1)} %reshape.68), calls=%async_computation | async-start | bytes 3276800 | tf_op jit(solution)/shard_map/all_to_all | solution.py:107
  29.8 39.2 %all-to-all-done = bf16[16,200,200]{2,1,0:T(8,128)(2,1)S(1)} async-done(((bf16[16,200,200]{2,1,0:T(8,128)(2,1)}), bf16[16,200,200]{2,1,0:T(8,128)(2,1)S(1)}, u32[]{:S(2)}, u32[]{:S(2)}) %all-to-all-start) | async-done | bytes 1280032 | tf_op jit(solution)/shard_map/all_to_all | solution.py:107
  69.0 0.8 reshape.69
  69.8 1.1 copy.23
  71.0 0.9 gather_fusion.2
  72.1 1.1 copy.24
  73.1 1.2 gather_fusion.3
  74.5 0.6 copy.25
  75.2 1.3 reshape.71
  76.5 0.9 collective-permute-start
  77.4 1.1 collective-permute-start.2
  78.4 31.1 %collective-permute-done = bf16[800,800]{1,0:T(8,128)(2,1)S(1)} collective-permute-done((bf16[800,800]{1,0:T(8,128)(2,1)S(1)}, bf16[800,800]{1,0:T(8,128)(2,1)S(1)}, u32[]{:S(2)}, u32[]{:S(2)}) %collective-permute-start) | collective-permute-done | bytes 1280032 | tf_op jit(solution)/shard_map/ppermute | solution.py:9
  109.6 1.1 copy-done.3
  110.7 1.4 broadcast_select_fusion.6
  112.0 1.2 collective-permute-start.3
  113.7 32.2 %collective-permute-done.3 = bf16[800,800]{1,0:T(8,128)(2,1)} collective-permute-done((bf16[800,800]{1,0:T(8,128)(2,1)}, bf16[800,800]{1,0:T(8,128)(2,1)}, u32[]{:S(2)}, u32[]{:S(2)}) %collective-permute-start.3) | collective-permute-done | bytes 1280032 | tf_op jit(solution)/shard_map/ppermute | solution.py:9
  145.9 1.5 broadcast_select_fusion.7
  147.5 1.4 collective-permute-start.5
  148.9 29.8 %collective-permute-done.1 = bf16[800,800]{1,0:T(8,128)(2,1)S(1)} collective-permute-done((bf16[800,800]{1,0:T(8,128)(2,1)S(1)}, bf16[800,800]{1,0:T(8,128)(2,1)S(1)}, u32[]{:S(2)}, u32[]{:S(2)}) %collective-permute-start.1) | collective-permute-done | bytes 1280032 | tf_op jit(solution)/shard_map/ppermute | solution.py:9
  178.9 1.5 collective-permute-start.4
  180.4 31.6 %collective-permute-done.4 = bf16[800,800]{1,0:T(8,128)(2,1)S(1)} collective-permute-done((bf16[800,800]{1,0:T(8,128)(2,1)S(1)}, bf16[800,800]{1,0:T(8,128)(2,1)S(1)}, u32[]{:S(2)}, u32[]{:S(2)}) %collective-permute-start.4) | collective-permute-done | bytes 1280032 | tf_op jit(solution)/shard_map/ppermute | solution.py:9
  212.1 1.8 fusion.4
  213.9 3.5 convolution_add_fusion.1
  218.3 2.2 mul.77
  220.5 76.9 %all-reduce.3.cloned.1.call-done = f32[800,800]{1,0:T(8,128)} async-done(((f32[800,800]{1,0:T(8,128)}), f32[800,800]{1,0:T(8,128)}) %all-reduce.3.cloned.1.call-update) | async-done | bytes 2560016 | tf_op jit(solution)/shard_map/psum | solution.py:112
  297.4 2.9 multiply_convert_fusion.1
  300.4 3.4 collective-permute-start.6
  303.8 30.7 %collective-permute-done.6 = bf16[800,800]{1,0:T(8,128)(2,1)S(1)} collective-permute-done((bf16[800,800]{1,0:T(8,128)(2,1)S(1)}, bf16[800,800]{1,0:T(8,128)(2,1)S(1)}, u32[]{:S(2)}, u32[]{:S(2)}) %collective-permute-start.6) | collective-permute-done | bytes 1280032 | tf_op jit(solution)/shard_map/ppermute | solution.py:9
  334.6 1.6 collective-permute-start.7
  336.2 62.3 %collective-permute-done.7 = bf16[800,800]{1,0:T(8,128)(2,1)S(1)} collective-permute-done((bf16[800,800]{1,0:T(8,128)(2,1)S(1)}, bf16[800,800]{1,0:T(8,128)(2,1)S(1)}, u32[]{:S(2)}, u32[]{:S(2)}) %collective-permute-start.7) | collective-permute-done | bytes 1280032 | tf_op jit(solution)/shard_map/ppermute | solution.py:9
  398.7 2.5 collective-permute-start.8
  401.3 30.9 %collective-permute-done.8 = bf16[800,800]{1,0:T(8,128)(2,1)S(1)} collective-permute-done((bf16[800,800]{1,0:T(8,128)(2,1)S(1)}, bf16[800,800]{1,0:T(8,128)(2,1)S(1)}, u32[]{:S(2)}, u32[]{:S(2)}) %collective-permute-start.8) | collective-permute-done | bytes 1280032 | tf_op jit(solution)/shard_map/ppermute | solution.py:9
  432.1 1.8 fusion.5
  433.9 3.4 convolution_add_fusion
  437.3 0.7 copy-done.6
  438.3 2.2 mul.84
  440.5 1.0 sort.79
  441.4 1.0 sort.80
  442.5 75.7 %all-reduce.5.cloned.1.call-done = f32[800,800]{1,0:T(8,128)} async-done(((f32[800,800]{1,0:T(8,128)}), f32[800,800]{1,0:T(8,128)}) %all-reduce.5.cloned.1.call-update) | async-done | bytes 2560016 | tf_op jit(solution)/shard_map/psum | solution.py:116
  518.1 3.6 multiply_convert_fusion
  521.7 2.0 reshape.72
  523.7 0.9 gather_fusion.4
  524.8 1.1 copy.26
  525.9 1.2 gather_fusion.5
  527.3 1.3 copy.33
  528.5 1.9 reshape.74
  530.4 5.6 all-to-all-start.1
  536.5 39.2 %all-to-all-done.1 = bf16[16,200,200]{2,1,0:T(8,128)(2,1)S(1)} async-done(((bf16[16,200,200]{2,1,0:T(8,128)(2,1)}), bf16[16,200,200]{2,1,0:T(8,128)(2,1)S(1)}, u32[]{:S(2)}, u32[]{:S(2)}) %all-to-all-start.1) | async-done | bytes 1280032 | tf_op jit(solution)/shard_map/all_to_all | solution.py:121
  575.7 0.8 reshape.75
  576.5 1.1 copy.28
  577.7 0.9 gather_fusion.6
  578.7 1.1 copy.29
  579.8 1.2 gather_fusion.7
  581.9 2.1 reshape.77
  (70 shorter events, 5.8 us)
Async XLA Ops:
  6.5 8.5 %copy-start.4 = (s32[8,8]{1,0:T(8,128)S(1)}, s32[8,8]{1,0:T(8,128)}, u32[]{:S(2)}) copy-start(s32[8,8]{1,0:T(8,128)} %param.10) | copy-start | bytes 772
  22.0 47.0 %all-to-all-start = ((bf16[16,200,200]{2,1,0:T(8,128)(2,1)}), bf16[16,200,200]{2,1,0:T(8,128)(2,1)S(1)}, u32[]{:S(2)}, u32[]{:S(2)}) async-start(bf16[16,200,200]{2,1,0:T(8,128)(2,1)} %reshape.68), calls=%async_computation | async-start | bytes 3276800 | tf_op jit(solution)/shard_map/all_to_all | solution.py:107
  29.4 268.1 %all-reduce.3.cloned.1.call-start = ((), (), s32[]{:S(2)}) async-start(), calls=%async_computation.2 | async-start | bytes 5734400 | tf_op jit(solution)/shard_map/psum | solution.py:112
  76.5 33.1 %collective-permute-start = (bf16[800,800]{1,0:T(8,128)(2,1)S(1)}, bf16[800,800]{1,0:T(8,128)(2,1)S(1)}, u32[]{:S(2)}, u32[]{:S(2)}) collective-permute-start(bf16[800,800]{1,0:T(8,128)(2,1)S(1)} %reshape.71), channel_id=1, source_target_pairs={{0,3},{1,0},{2,1},{3,2},{4,7},{5,4},{6,5},{7,6},{8,11},{9,8},{10,9... | collective-permute-start | bytes 3840008 | tf_op jit(solution)/shard_map/ppermute | solution.py:9
  77.4 33.3 %collective-permute-start.2 = (bf16[800,800]{1,0:T(8,128)(2,1)S(1)}, bf16[800,800]{1,0:T(8,128)(2,1)}, u32[]{:S(2)}, u32[]{:S(2)}) collective-permute-start(bf16[800,800]{1,0:T(8,128)(2,1)S(1)} %reshape.71), channel_id=1, source_target_pairs={{0,12},{4,0},{8,4},{12,8},{1,13},{5,1},{9,5},{13,9},{2,14},{6,2},{... | collective-permute-start | bytes 3840008 | tf_op jit(solution)/shard_map/ppermute | solution.py:9
  109.6 1.1 copy-start.3
  112.0 33.9 %collective-permute-start.3 = (bf16[800,800]{1,0:T(8,128)(2,1)}, bf16[800,800]{1,0:T(8,128)(2,1)}, u32[]{:S(2)}, u32[]{:S(2)}) collective-permute-start(bf16[800,800]{1,0:T(8,128)(2,1)} %get-tuple-element.33), channel_id=1, source_target_pairs={{0,8},{4,12},{8,0},{12,4},{1,9},{5,13},{9,1},{13,5},{2,10},{6,14},... | collective-permute-start | bytes 3840008 | tf_op jit(solution)/shard_map/ppermute | solution.py:9
  113.2 65.5 %collective-permute-start.1 = (bf16[800,800]{1,0:T(8,128)(2,1)S(1)}, bf16[800,800]{1,0:T(8,128)(2,1)S(1)}, u32[]{:S(2)}, u32[]{:S(2)}) collective-permute-start(bf16[800,800]{1,0:T(8,128)(2,1)S(1)} %get-tuple-element.34), channel_id=1, source_target_pairs={{0,2},{1,3},{2,0},{3,1},{4,6},{5,7},{6,4},{7,5},{8,10},{9,11},{10,... | collective-permute-start | bytes 3840008 | tf_op jit(solution)/shard_map/ppermute | solution.py:9
  147.5 66.4 %copy-start.1 = (bf16[800,800]{1,0:T(8,128)(2,1)}, bf16[800,800]{1,0:T(8,128)(2,1)S(1)}, u32[]{:S(2)}) copy-start(bf16[800,800]{1,0:T(8,128)(2,1)S(1)} %broadcast_select_fusion.7) | copy-start | bytes 3840004
  147.5 33.0 %collective-permute-start.5 = (bf16[800,800]{1,0:T(8,128)(2,1)S(1)}, bf16[800,800]{1,0:T(8,128)(2,1)S(1)}, u32[]{:S(2)}, u32[]{:S(2)}) collective-permute-start(bf16[800,800]{1,0:T(8,128)(2,1)S(1)} %broadcast_select_fusion.7), channel_id=1, source_target_pairs={{0,12},{4,0},{8,4},{12,8},{1,13},{5,1},{9,5},{13,9},{2,14},{6,2},{... | collective-permute-start | bytes 3840008 | tf_op jit(solution)/shard_map/ppermute | solution.py:9
  178.9 33.2 %collective-permute-start.4 = (bf16[800,800]{1,0:T(8,128)(2,1)S(1)}, bf16[800,800]{1,0:T(8,128)(2,1)S(1)}, u32[]{:S(2)}, u32[]{:S(2)}) collective-permute-start(bf16[800,800]{1,0:T(8,128)(2,1)S(1)} %broadcast_select_fusion.11), channel_id=1, source_target_pairs={{0,3},{1,0},{2,1},{3,2},{4,7},{5,4},{6,5},{7,6},{8,11},{9,8},{10,9... | collective-permute-start | bytes 3840008 | tf_op jit(solution)/shard_map/ppermute | solution.py:9
  180.4 33.4 %copy-start.7 = (bf16[800,800]{1,0:T(8,128)(2,1)}, bf16[800,800]{1,0:T(8,128)(2,1)S(1)}, u32[]{:S(2)}) copy-start(bf16[800,800]{1,0:T(8,128)(2,1)S(1)} %collective-permute-done.5) | copy-start | bytes 3840004
  217.4 0.7 copy-start.5
  217.4 300.7 %all-reduce.5.cloned.1.call-start = ((), (), s32[]{:S(2)}) async-start(), calls=%async_computation.3 | async-start | bytes 5734400 | tf_op jit(solution)/shard_map/psum | solution.py:116
  300.4 34.2 %copy-start = (bf16[800,800]{1,0:T(8,128)(2,1)}, bf16[800,800]{1,0:T(8,128)(2,1)S(1)}, u32[]{:S(2)}) copy-start(bf16[800,800]{1,0:T(8,128)(2,1)S(1)} %multiply_convert_fusion.1) | copy-start | bytes 3840004
  300.4 34.1 %collective-permute-start.6 = (bf16[800,800]{1,0:T(8,128)(2,1)S(1)}, bf16[800,800]{1,0:T(8,128)(2,1)S(1)}, u32[]{:S(2)}, u32[]{:S(2)}) collective-permute-start(bf16[800,800]{1,0:T(8,128)(2,1)S(1)} %multiply_convert_fusion.1), channel_id=1, source_target_pairs={{0,3},{1,0},{2,1},{3,2},{4,7},{5,4},{6,5},{7,6},{8,11},{9,8},{10,9... | collective-permute-start | bytes 3840008 | tf_op jit(solution)/shard_map/ppermute | solution.py:9
  334.6 97.5 %copy-start.8 = (bf16[800,800]{1,0:T(8,128)(2,1)S(1)}, bf16[800,800]{1,0:T(8,128)(2,1)}, u32[]{:S(2)}) copy-start(bf16[800,800]{1,0:T(8,128)(2,1)} %copy-done.7) | copy-start | bytes 3840004
  334.6 64.0 %collective-permute-start.7 = (bf16[800,800]{1,0:T(8,128)(2,1)S(1)}, bf16[800,800]{1,0:T(8,128)(2,1)S(1)}, u32[]{:S(2)}, u32[]{:S(2)}) collective-permute-start(bf16[800,800]{1,0:T(8,128)(2,1)S(1)} %broadcast_select_fusion.8), channel_id=1, source_target_pairs={{0,2},{1,3},{2,0},{3,1},{4,6},{5,7},{6,4},{7,5},{8,10},{9,11},{10,... | collective-permute-start | bytes 3840008 | tf_op jit(solution)/shard_map/ppermute | solution.py:9
  398.7 35.2 %copy-start.2 = (bf16[800,800]{1,0:T(8,128)(2,1)S(1)}, bf16[800,800]{1,0:T(8,128)(2,1)}, u32[]{:S(2)}) copy-start(bf16[800,800]{1,0:T(8,128)(2,1)} %copy-done.1) | copy-start | bytes 3840004
  398.7 33.4 %collective-permute-start.8 = (bf16[800,800]{1,0:T(8,128)(2,1)S(1)}, bf16[800,800]{1,0:T(8,128)(2,1)S(1)}, u32[]{:S(2)}, u32[]{:S(2)}) collective-permute-start(bf16[800,800]{1,0:T(8,128)(2,1)S(1)} %broadcast_select_fusion.10), channel_id=1, source_target_pairs={{0,3},{1,0},{2,1},{3,2},{4,7},{5,4},{6,5},{7,6},{8,11},{9,8},{10,9... | collective-permute-start | bytes 3840008 | tf_op jit(solution)/shard_map/ppermute | solution.py:9
  437.3 0.7 copy-start.6
  530.4 45.2 %all-to-all-start.1 = ((bf16[16,200,200]{2,1,0:T(8,128)(2,1)}), bf16[16,200,200]{2,1,0:T(8,128)(2,1)S(1)}, u32[]{:S(2)}, u32[]{:S(2)}) async-start(bf16[16,200,200]{2,1,0:T(8,128)(2,1)} %reshape.74), calls=%async_computation.1 | async-start | bytes 3276800 | tf_op jit(solution)/shard_map/all_to_all | solution.py:121
Sparse Core Ops, SparseCore 0:
  217.5 79.8 all-reduce.2
  437.5 80.6 all-reduce.4
where the time goes:
time: 591 us
  waiting for transfers between devices  480 us (81%)
  local copies, waits for them, and re-layouts  40.1 us (7%)
  starting transfers between devices  27.2 us (5%)
  other arithmetic  19.7 us (3%)
  between operations  13.9 us (2%)
  matrix products  10.5 us (2%)
    ppermute x9, waiting for transfers between devices, passed_along(): lax.ppermute(array, axis, [(i, (i + by) % count) for i in range(count)])  249 us
    psum x1, waiting for transfers between devices, per_device(): square_full = lax.psum(square_part, 'layer')  76.9 us
    psum x1, waiting for transfers between devices, per_device(): cube = lax.psum(cube_part, 'layer')  75.7 us
    all_to_all x1, waiting for transfers between devices, per_device(): lax.all_to_all(outgoing, ('row', 'col'), split_axis=0, concat_axis=0, til...  39.2 us
    all_to_all x1, waiting for transfers between devices, per_device(): lax.all_to_all(pieces, ('row', 'col'), split_axis=0, concat_axis=0, tiled...  39.2 us
    ppermute x9, starting transfers between devices, passed_along(): lax.ppermute(array, axis, [(i, (i + by) % count) for i in range(count)])  14.1 us
  transfers between devices with their start and end apart: 13, of which 11 were waited for; matrix products, arithmetic and copies ran while one was open for 2% of the time, Pallas kernels for 0%

commit v1 on v0

v1 whole, which is shorter than its diff:
```python
import functools

import jax
import jax.numpy as jnp
from jax import lax
from jax.experimental import pallas as pl
from jax.experimental.pallas import tpu as pltpu
from jax.sharding import PartitionSpec as P

MESH = pl.DeviceIdType.MESH
LANES = 128


def row_chunks(rows):
    first = (rows // 32 + 1) * 16
    return ((0, first), (first, rows - first))


def copy_to(src, dst, send_sem, recv_sem, device):
    return pltpu.make_async_remote_copy(
        src_ref=src,
        dst_ref=dst,
        send_sem=send_sem,
        recv_sem=recv_sem,
        device_id=device,
        device_id_type=MESH,
    )


class Line:
    def __init__(self, part, send, recv, pos, count, device):
        self.part, self.send, self.recv = part, send, recv
        self.pos, self.count, self.device = pos, count, device

    def copy(self, k, way):
        part = self.part(k)
        target = self.device(self.pos + (1, -1)[way])
        return copy_to(part, part, self.send.at[way, k], self.recv.at[k], target)

    def has(self, way):
        return (self.pos < self.count - 1, self.pos > 0)[way]

    def start(self, k, way):
        @pl.when(self.has(way))
        def _():
            self.copy(k, way).start()

    def start_own(self):
        self.start(self.pos, 0)
        self.start(self.pos, 1)

    def step(self, s, then=None):
        for way in (0, 1):
            k = self.pos + (-s, s)[way]

            @pl.when(jnp.logical_and(k >= 0, k < self.count))
            def _():
                self.copy(k, 1 - way).wait_recv()
                self.start(k, way)
                if then is not None:
                    then(k)

    def wait_sends(self):
        for k in range(self.count):
            for way in (0, 1):
                held = (k <= self.pos, k >= self.pos)[way]

                @pl.when(jnp.logical_and(held, self.has(way)))
                def _():
                    self.copy(k, way).wait_send()


def spread(size, width, blocks, along):
    shape = (size, blocks) if along == 0 else (blocks, size)
    element = lax.broadcasted_iota(jnp.int32, shape, along)
    block = lax.broadcasted_iota(jnp.int32, shape, 1 - along)
    inside = jnp.logical_and(element >= block * width, element < (block + 1) * width)
    return inside.astype(jnp.float32)


def dot(a, b):
    return jnp.dot(a, b, preferred_element_type=jnp.float32)


def kernel(n, layers, dens, dmask, smask, rmask, perm, out, B, A, S, acc, keep_s, keep_r, G,
           m_send, m_recv, g_send, g_recv, b_send, b_recv, t_send, t_recv,
           a_send, a_recv, s_send, s_recv, x_send, x_recv):
    l = lax.axis_index("layer")
    r = lax.axis_index("row")
    c = lax.axis_index("col")
    size = dens.shape[0]
    blocks = dmask.shape[0]
    width = size // blocks
    half = size // layers
    half_blocks = blocks // layers
    chunks = row_chunks(half)
    y, core = r // 2, r % 2
    ny = n // 2
    twin = {"row": y * 2 + 1 - core}
    other = {"layer": 1 - l}

    barrier = pltpu.get_barrier_semaphore()
    for step in range(1, n):
        pl.semaphore_signal(barrier, 1, device_id={"row": (r + step) % n}, device_id_type=MESH)
    pl.semaphore_signal(barrier, 1, device_id=other, device_id_type=MESH)

    @pl.when(c > 0)
    def _():
        pl.semaphore_signal(barrier, 1, device_id={"col": c - 1}, device_id_type=MESH)

    @pl.when(c < n - 1)
    def _():
        pl.semaphore_signal(barrier, 1, device_id={"col": c + 1}, device_id_type=MESH)

    lane = lax.broadcasted_iota(jnp.int32, (blocks, LANES), 1)
    line_no = lax.broadcasted_iota(jnp.int32, (blocks, LANES), 0)
    put_s = (lane == c * blocks + line_no).astype(jnp.float32)
    put_r = (lane == LANES // 2 + c * blocks + line_no).astype(jnp.float32)
    mine = pl.ds(pl.multiple_of(r * blocks, 8), blocks)
    G[c, mine, :] = dot(smask[...].astype(jnp.float32), put_s) + dot(rmask[...].astype(jnp.float32), put_r)

    rows_of = dot(spread(size, width, blocks, 0), dmask[...].astype(jnp.float32))
    keep = dot(rows_of, spread(size, width, blocks, 1))
    masked = jnp.where(keep > 0.5, dens[...], jnp.zeros_like(dens[...]))
    B[r] = masked
    top = pl.ds(pl.multiple_of(l * half, 16), half)
    A[c] = B[r, top, :]

    ends = jnp.where(c == 0, 1, 0) + jnp.where(c == n - 1, 1, 0)
    pl.semaphore_wait(barrier, n + 2 - ends)

    def mask_copy(step):
        place = G.at[c, mine]
        return copy_to(place, place, m_send.at[step], m_recv.at[step], {"row": (r + step) % n})

    for step in range(1, n):
        mask_copy(step).start()

    def at_col(k):
        return {"col": k}

    a_lines, s_lines = [], []
    for j, (off, rows) in enumerate(chunks):
        a_lines.append(Line(lambda k, off=off, rows=rows: A.at[k, pl.ds(off, rows)],
                            a_send.at[j], a_recv.at[j], c, n, at_col))
        s_lines.append(Line(lambda k, off=off, rows=rows: S.at[k, pl.ds(off, rows)],
                            s_send.at[j], s_recv.at[j], c, n, at_col))
    g_line = Line(lambda k: G.at[k], g_send, g_recv, c, n, at_col)
    b_line = Line(lambda k: B.at[k * 2 + core], b_send, b_recv, y, ny, lambda k: {"row": k * 2 + core})

    def twin_copy(k):
        place = B.at[k * 2 + core]
        return copy_to(place, place, t_send.at[k], t_recv.at[k], twin)

    for line in a_lines:
        line.start_own()
    b_line.start_own()
    twin_copy(y).start()

    for step in range(1, n):
        mask_copy(step).wait_recv()
    g_line.start_own()
    for line in a_lines:
        line.step(1)
    g_line.step(1)
    for s in range(1, ny):
        b_line.step(s, lambda k: twin_copy(k).start())
    for s in range(2, n):
        g_line.step(s)
        for line in a_lines if s < n - 1 else ():
            line.step(s)
    for k in range(ny):
        place = B.at[k * 2 + 1 - core]
        copy_to(place, place, t_send.at[k], t_recv.at[k], twin).wait_recv()

    whole = G[0]
    for k in range(1, n):
        whole = whole + G[k]
    row_at = lax.broadcasted_iota(jnp.int32, (half, n * blocks), 0)
    row_to = jnp.zeros((half, n * blocks), jnp.int32)
    for t in range(half_blocks):
        row_to = jnp.where(row_at >= t * width, perm[r * blocks + l * half_blocks + t], row_to)
    pick_rows = (row_to == lax.broadcasted_iota(jnp.int32, (half, n * blocks), 1)).astype(jnp.float32)
    picked = dot(pick_rows, whole)
    col_at = lax.broadcasted_iota(jnp.int32, (LANES, size), 1)
    col_to = jnp.zeros((LANES, size), jnp.int32)
    for t in range(blocks):
        col_to = jnp.where(col_at >= t * width, perm[c * blocks + t], col_to)
    slot = lax.broadcasted_iota(jnp.int32, (LANES, size), 0)
    keep_s[...] = dot(picked, (col_to == slot).astype(jnp.float32))
    keep_r[...] = dot(picked, (col_to + LANES // 2 == slot).astype(jnp.float32))

    def product(left, off, rows):
        acc[0:rows, :] = jnp.zeros((rows, size), jnp.float32)

        def body(k, carry):
            acc[0:rows, :] += dot(left[k, off:off + rows, :], B[k])
            return carry

        lax.fori_loop(0, n, body, 0)

    for j, (off, rows) in enumerate(chunks):
        a_lines[j].step(n - 1)
        product(A, off, rows)
        value = jnp.where(keep_s[off:off + rows, :] > 0.5, acc[0:rows, :], 0.0)
        S[c, off:off + rows, :] = value.astype(jnp.bfloat16)
        s_lines[j].start_own()

    def result_copy(j):
        off, rows = chunks[j]
        place = out.at[pl.ds(pl.multiple_of(l * half + off, 16), rows)]
        return copy_to(place, place, x_send.at[j], x_recv.at[j], other)

    for s in range(1, n - 1):
        for line in s_lines:
            line.step(s)
    for j, (off, rows) in enumerate(chunks):
        s_lines[j].step(n - 1)
        product(S, off, rows)
        value = 3.0 * S[c, off:off + rows, :].astype(jnp.float32) - 2.0 * acc[0:rows, :]
        value = jnp.where(keep_r[off:off + rows, :] > 0.5, value, 0.0)
        out[pl.ds(pl.multiple_of(l * half + off, 16), rows), :] = value.astype(jnp.bfloat16)
        result_copy(j).start()

    for j, (off, rows) in enumerate(chunks):
        place = out.at[pl.ds(pl.multiple_of((1 - l) * half + off, 16), rows)]
        copy_to(place, place, x_send.at[j], x_recv.at[j], other).wait_recv()
        result_copy(j).wait_send()
    for line in (g_line, b_line, *a_lines, *s_lines):
        line.wait_sends()
    for k in range(ny):
        twin_copy(k).wait_send()
    for step in range(1, n):
        mask_copy(step).wait_send()


def per_device(n, layers, density, density_mask, square_mask, result_mask, block_perm):
    size = density.shape[0]
    half = size // layers
    blocks = density_mask.shape[0]
    pieces = row_chunks(half)
    count = len(pieces)
    most = max(rows for _, rows in pieces)
    bf16, f32 = jnp.bfloat16, jnp.float32
    dma = pltpu.SemaphoreType.DMA
    vmem = pl.BlockSpec(memory_space=pltpu.VMEM)
    return pl.pallas_call(
        functools.partial(kernel, n, layers),
        out_shape=jax.ShapeDtypeStruct((size, size), bf16),
        in_specs=[vmem] * 4 + [pl.BlockSpec(memory_space=pltpu.SMEM)],
        out_specs=vmem,
        scratch_shapes=[
            pltpu.VMEM((n, size, size), bf16),
            pltpu.VMEM((n, half, size), bf16),
            pltpu.VMEM((n, half, size), bf16),
            pltpu.VMEM((most, size), f32),
            pltpu.VMEM((half, size), f32),
            pltpu.VMEM((half, size), f32),
            pltpu.VMEM((n, n * blocks, LANES), f32),
            dma((n,)), dma((n,)),
            dma((2, n)), dma((n,)),
            dma((2, n // 2)), dma((n // 2,)),
            dma((n // 2,)), dma((n // 2,)),
            dma((count, 2, n)), dma((count, n)),
            dma((count, 2, n)), dma((count, n)),
            dma((count,)), dma((count,)),
        ],
        compiler_params=pltpu.CompilerParams(
            collective_id=0, has_side_effects=True, vmem_limit_bytes=56 * 2**20
        ),
        cost_estimate=pl.CostEstimate(
            flops=4 * n * half * size * size, bytes_accessed=4 * size * size, transcendentals=0
        ),
    )(density, density_mask, square_mask, result_mask, block_perm)


def solution(mesh):
    in_specs = (P("row", "col"), P("row", "col"), P("row", "col"), P("row", "col"), P())
    return jax.shard_map(
        functools.partial(per_device, mesh.shape["row"], mesh.shape["layer"]),
        mesh=mesh,
        in_specs=in_specs,
        out_specs=P("row", "col"),
        check_vma=False,
    )
```

time: 591 us -> 119 us (0.20)
  waiting for transfers between devices: 480 us -> 0 us
  Pallas kernels: 0 us -> 116 us
  local copies, waits for them, and re-layouts: 40.1 us -> 2.57 us
  starting transfers between devices: 27.2 us -> 0 us
  other arithmetic: 19.7 us -> 0 us
  between operations: 13.9 us -> 0.01 us
  matrix products: 10.5 us -> 0 us
    ppermute x9 -> x0, waiting for transfers between devices: 249 us -> none  [passed_along(): lax.ppermute(array, axis, [(i, (i + by) % count) for i in range(count)])]
    psum x2 -> x0, waiting for transfers between devices: 153 us -> none  [the longest x1 76.9 us: per_device(): square_full = lax.psum(square_part, 'layer')]
    pallas_call x0 -> x1, Pallas kernels: none -> 116 us  [per_device(): pl.pallas_call(functools.partial(kernel, n, layers), out_shape=jax.ShapeD...]
    all_to_all x2 -> x0, waiting for transfers between devices: 78.3 us -> none  [the longest x1 39.2 us: per_device(): lax.all_to_all(outgoing, ('row', 'col'), split_axis=0, concat_axis=0, til...]
    reshape x12 -> x0, local copies, waits for them, and re-layouts: 19.1 us -> none  [the longest x4 3.92 us: assemble(): shaped = received.reshape(groups, groups, per_pair, width, per_pair, width)]
    ppermute x9 -> x0, starting transfers between devices: 14.1 us -> none  [passed_along(): lax.ppermute(array, axis, [(i, (i + by) % count) for i in range(count)])]
    all_to_all x2 -> x0, starting transfers between devices: 13 us -> none  [the longest x1 7.39 us: per_device(): lax.all_to_all(pieces, ('row', 'col'), split_axis=0, concat_axis=0, tiled...]
    dot_general x4 -> x0, matrix products: 10.5 us -> none  [the longest x2 5.26 us: square_pass(): total = total + jnp.dot(left, right, preferred_element_type=jnp.float32)]
  transfers between devices with their start and end apart: 13 -> 0, of which waited for: 11 -> 0; matrix products, arithmetic and copies ran while one was open for 2% -> 0% of each run, Pallas kernels for 0% -> 0%
where the time goes in v1:
time: 119 us
  Pallas kernels  116 us (97%)
  local copies, waits for them, and re-layouts  2.57 us (2%)
    pallas_call x1, Pallas kernels, per_device(): pl.pallas_call(functools.partial(kernel, n, layers), out_shape=jax.ShapeD...  116 us
    unnamed x1, local copies, waits for them, and re-layouts  2.57 us

profile of v1, /device:TPU:0, one launch (start us, length us, event | category | flops | bytes accessed | tf_op | source)
XLA Modules:
  0.0 118.6 jit_solution(2597825319853157925)
XLA Ops:
  0.0 116.0 %shard_map.55 = bf16[800,800]{1,0:T(8,128)(2,1)} custom-call(bf16[800,800]{1,0:T(8,128)(2,1)} %dens.1, s32[8,8]{1,0:T(8,128)} %dmask.1, s32[8,8]{1,0:T(8,128)} %smask.1, s32[8,8]{1,0:T(8,128)} %rmask.1, s32[32]{0:T(128)} %perm.1), custom_call_target="tpu_custom_call" | custom-call | flops 4096000000 | bytes 2560000 | tf_op jit(solution)/shard_map/pallas_call | solution.py:247
  116.0 2.6 %copy.7 = bf16[800,800]{1,0:T(8,128)(2,1)} copy(bf16[800,800]{1,0:T(8,128)(2,1)} %shard_map.55) | data formatting | bytes 2560000

commit v2 on v1

--- a/solution.py
+++ b/solution.py
@@ -11,9 +11,20 @@
 LANES = 128
 
 
+CHUNKS = 3
+
+
 def row_chunks(rows):
-    first = (rows // 32 + 1) * 16
-    return ((0, first), (first, rows - first))
+    groups = rows // 16
+    sizes = [16 * (groups // CHUNKS + (j < groups % CHUNKS)) for j in range(CHUNKS)]
+    return tuple((sum(sizes[:j]), sizes[j]) for j in range(CHUNKS))
+
+
+def tail_groups(rows, tail):
+    per = LANES // tail
+    high = -(-rows // (16 * per)) * 16
+    assert rows % high == 0
+    return high, rows // high
 
 
 def copy_to(src, dst, send_sem, recv_sem, device):
@@ -82,9 +93,33 @@
     return jnp.dot(a, b, preferred_element_type=jnp.float32)
 
 
-def kernel(n, layers, dens, dmask, smask, rmask, perm, out, B, A, S, acc, keep_s, keep_r, G,
+def shift(tail, g, wide):
+    shape = (tail, LANES) if wide else (LANES, tail)
+    narrow = lax.broadcasted_iota(jnp.int32, shape, 1 - wide)
+    lane = lax.broadcasted_iota(jnp.int32, shape, int(wide))
+    return (lane == g * tail + narrow).astype(jnp.bfloat16)
+
+
+def pack(src, k, off, rows, dst, j, main, tail):
+    high, count = tail_groups(rows, tail)
+    total = jnp.zeros((high, LANES), jnp.float32)
+    for g in range(count):
+        at = off + g * high
+        total = total + dot(src[k, at:at + high, main:main + tail], shift(tail, g, True))
+    dst[k, j, 0:high, :] = total.astype(jnp.bfloat16)
+
+
+def unpack(src, k, j, off, rows, dst, main, tail):
+    high, count = tail_groups(rows, tail)
+    packed = src[k, j, 0:high, :]
+    for g in range(count):
+        at = off + g * high
+        dst[k, at:at + high, main:main + tail] = dot(packed, shift(tail, g, False)).astype(jnp.bfloat16)
+
+
+def kernel(n, layers, dens, dmask, smask, rmask, perm, out, B, A, S, AT, ST, acc, keep_s, keep_r, G,
            m_send, m_recv, g_send, g_recv, b_send, b_recv, t_send, t_recv,
-           a_send, a_recv, s_send, s_recv, x_send, x_recv):
+           a_send, a_recv, s_send, s_recv, at_send, at_recv, st_send, st_recv, x_send, x_recv):
     l = lax.axis_index("layer")
     r = lax.axis_index("row")
     c = lax.axis_index("col")
@@ -94,6 +129,8 @@
     half = size // layers
     half_blocks = blocks // layers
     chunks = row_chunks(half)
+    tail = size % LANES
+    main = size - tail
     y, core = r // 2, r % 2
     ny = n // 2
     twin = {"row": y * 2 + 1 - core}
@@ -125,6 +162,8 @@
     B[r] = masked
     top = pl.ds(pl.multiple_of(l * half, 16), half)
     A[c] = B[r, top, :]
+    for j, (off, rows) in enumerate(chunks):
+        pack(A, c, off, rows, AT, j, main, tail)
 
     ends = jnp.where(c == 0, 1, 0) + jnp.where(c == n - 1, 1, 0)
     pl.semaphore_wait(barrier, n + 2 - ends)
@@ -139,12 +178,29 @@
     def at_col(k):
         return {"col": k}
 
-    a_lines, s_lines = [], []
-    for j, (off, rows) in enumerate(chunks):
-        a_lines.append(Line(lambda k, off=off, rows=rows: A.at[k, pl.ds(off, rows)],
-                            a_send.at[j], a_recv.at[j], c, n, at_col))
-        s_lines.append(Line(lambda k, off=off, rows=rows: S.at[k, pl.ds(off, rows)],
-                            s_send.at[j], s_recv.at[j], c, n, at_col))
+    def lines_of(whole_part, tail_part, send, recv, tail_send, tail_recv):
+        made = []
+        for j, (off, rows) in enumerate(chunks):
+            high, _ = tail_groups(rows, tail)
+            made.append((
+                Line(lambda k, j=j, high=high: tail_part.at[k, j, pl.ds(0, high)],
+                     tail_send.at[j], tail_recv.at[j], c, n, at_col),
+                Line(lambda k, off=off, rows=rows: whole_part.at[k, pl.ds(off, rows), pl.ds(0, main)],
+                     send.at[j], recv.at[j], c, n, at_col),
+            ))
+        return made
+
+    a_lines = lines_of(A, AT, a_send, a_recv, at_send, at_recv)
+    s_lines = lines_of(S, ST, s_send, s_recv, st_send, st_recv)
+
+    def start_own(pair):
+        for line in pair:
+            line.start_own()
+
+    def step_all(pair, s):
+        for line in pair:
+            line.step(s)
+
     g_line = Line(lambda k: G.at[k], g_send, g_recv, c, n, at_col)
     b_line = Line(lambda k: B.at[k * 2 + core], b_send, b_recv, y, ny, lambda k: {"row": k * 2 + core})
 
@@ -152,23 +208,23 @@
         place = B.at[k * 2 + core]
         return copy_to(place, place, t_send.at[k], t_recv.at[k], twin)
 
-    for line in a_lines:
-        line.start_own()
+    for pair in a_lines:
+        start_own(pair)
     b_line.start_own()
     twin_copy(y).start()
 
     for step in range(1, n):
         mask_copy(step).wait_recv()
     g_line.start_own()
-    for line in a_lines:
-        line.step(1)
+    for pair in a_lines:
+        step_all(pair, 1)
     g_line.step(1)
     for s in range(1, ny):
         b_line.step(s, lambda k: twin_copy(k).start())
     for s in range(2, n):
         g_line.step(s)
-        for line in a_lines if s < n - 1 else ():
-            line.step(s)
+        for pair in a_lines if s < n - 1 else ():
+            step_all(pair, s)
     for k in range(ny):
         place = B.at[k * 2 + 1 - core]
         copy_to(place, place, t_send.at[k], t_recv.at[k], twin).wait_recv()
@@ -190,21 +246,26 @@
     keep_s[...] = dot(picked, (col_to == slot).astype(jnp.float32))
     keep_r[...] = dot(picked, (col_to + LANES // 2 == slot).astype(jnp.float32))
 
-    def product(left, off, rows):
+    def product(left, tails, j, off, rows):
         acc[0:rows, :] = jnp.zeros((rows, size), jnp.float32)
 
         def body(k, carry):
+            @pl.when(k != c)
+            def _():
+                unpack(tails, k, j, off, rows, left, main, tail)
+
             acc[0:rows, :] += dot(left[k, off:off + rows, :], B[k])
             return carry
 
         lax.fori_loop(0, n, body, 0)
 
     for j, (off, rows) in enumerate(chunks):
-        a_lines[j].step(n - 1)
-        product(A, off, rows)
+        step_all(a_lines[j], n - 1)
+        product(A, AT, j, off, rows)
         value = jnp.where(keep_s[off:off + rows, :] > 0.5, acc[0:rows, :], 0.0)
         S[c, off:off + rows, :] = value.astype(jnp.bfloat16)
-        s_lines[j].start_own()
+        pack(S, c, off, rows, ST, j, main, tail)
+        start_own(s_lines[j])
 
     def result_copy(j):
         off, rows = chunks[j]
@@ -212,11 +273,11 @@
         return copy_to(place, place, x_send.at[j], x_recv.at[j], other)
 
     for s in range(1, n - 1):
-        for line in s_lines:
-            line.step(s)
+        for pair in s_lines:
+            step_all(pair, s)
     for j, (off, rows) in enumerate(chunks):
-        s_lines[j].step(n - 1)
-        product(S, off, rows)
+        step_all(s_lines[j], n - 1)
+        product(S, ST, j, off, rows)
         value = 3.0 * S[c, off:off + rows, :].astype(jnp.float32) - 2.0 * acc[0:rows, :]
         value = jnp.where(keep_r[off:off + rows, :] > 0.5, value, 0.0)
         out[pl.ds(pl.multiple_of(l * half + off, 16), rows), :] = value.astype(jnp.bfloat16)
@@ -226,7 +287,7 @@
         place = out.at[pl.ds(pl.multiple_of((1 - l) * half + off, 16), rows)]
         copy_to(place, place, x_send.at[j], x_recv.at[j], other).wait_recv()
         result_copy(j).wait_send()
-    for line in (g_line, b_line, *a_lines, *s_lines):
+    for line in (g_line, b_line, *(line for pair in (*a_lines, *s_lines) for line in pair)):
         line.wait_sends()
     for k in range(ny):
         twin_copy(k).wait_send()
@@ -241,6 +302,7 @@
     pieces = row_chunks(half)
     count = len(pieces)
     most = max(rows for _, rows in pieces)
+    high = max(tail_groups(rows, size % LANES)[0] for _, rows in pieces)
     bf16, f32 = jnp.bfloat16, jnp.float32
     dma = pltpu.SemaphoreType.DMA
     vmem = pl.BlockSpec(memory_space=pltpu.VMEM)
@@ -253,6 +315,8 @@
             pltpu.VMEM((n, size, size), bf16),
             pltpu.VMEM((n, half, size), bf16),
             pltpu.VMEM((n, half, size), bf16),
+            pltpu.VMEM((n, count, high, LANES), bf16),
+            pltpu.VMEM((n, count, high, LANES), bf16),
             pltpu.VMEM((most, size), f32),
             pltpu.VMEM((half, size), f32),
             pltpu.VMEM((half, size), f32),
@@ -261,6 +325,8 @@
             dma((2, n)), dma((n,)),
             dma((2, n // 2)), dma((n // 2,)),
             dma((n // 2,)), dma((n // 2,)),
+            dma((count, 2, n)), dma((count, n)),
+            dma((count, 2, n)), dma((count, n)),
             dma((count, 2, n)), dma((count, n)),
             dma((count, 2, n)), dma((count, n)),
             dma((count,)), dma((count,)),

time: 119 us -> 111 us (0.933)
  Pallas kernels: 116 us -> 108 us
    pallas_call x1, Pallas kernels: 116 us -> 108 us  [per_device(): pl.pallas_call(functools.partial(kernel, n, layers), out_shape=jax.ShapeD...]
where the time goes in v2:
time: 111 us
  Pallas kernels  108 us (97%)
  local copies, waits for them, and re-layouts  2.57 us (2%)
    pallas_call x1, Pallas kernels, per_device(): pl.pallas_call(functools.partial(kernel, n, layers), out_shape=jax.ShapeD...  108 us
    unnamed x1, local copies, waits for them, and re-layouts  2.57 us

profile of v2, /device:TPU:0, one launch (start us, length us, event | category | flops | bytes accessed | tf_op | source)
XLA Modules:
  0.0 110.7 jit_solution(10962396783258428893)
XLA Ops:
  0.0 108.1 %shard_map.55 = bf16[800,800]{1,0:T(8,128)(2,1)} custom-call(bf16[800,800]{1,0:T(8,128)(2,1)} %dens.1, s32[8,8]{1,0:T(8,128)} %dmask.1, s32[8,8]{1,0:T(8,128)} %smask.1, s32[8,8]{1,0:T(8,128)} %rmask.1, s32[32]{0:T(128)} %perm.1), custom_call_target="tpu_custom_call" | custom-call | flops 4096000000 | bytes 2560000 | tf_op jit(solution)/shard_map/pallas_call | solution.py:309
  108.1 2.6 %copy.7 = bf16[800,800]{1,0:T(8,128)(2,1)} copy(bf16[800,800]{1,0:T(8,128)(2,1)} %shard_map.55) | data formatting | bytes 2560000

commit v3 on v2

--- a/solution.py
+++ b/solution.py
@@ -219,12 +219,12 @@
     for pair in a_lines:
         step_all(pair, 1)
     g_line.step(1)
-    for s in range(1, ny):
-        b_line.step(s, lambda k: twin_copy(k).start())
     for s in range(2, n):
         g_line.step(s)
         for pair in a_lines if s < n - 1 else ():
             step_all(pair, s)
+        if s - 1 < ny:
+            b_line.step(s - 1, lambda k: twin_copy(k).start())
     for k in range(ny):
         place = B.at[k * 2 + 1 - core]
         copy_to(place, place, t_send.at[k], t_recv.at[k], twin).wait_recv()

time: 111 us -> 109 us (0.982)
  Pallas kernels: 108 us -> 106 us
    pallas_call x1, Pallas kernels: 108 us -> 106 us  [per_device(): pl.pallas_call(functools.partial(kernel, n, layers), out_shape=jax.ShapeD...]
where the time goes in v3:
time: 109 us
  Pallas kernels  106 us (97%)
  local copies, waits for them, and re-layouts  2.57 us (2%)
    pallas_call x1, Pallas kernels, per_device(): pl.pallas_call(functools.partial(kernel, n, layers), out_shape=jax.ShapeD...  106 us
    unnamed x1, local copies, waits for them, and re-layouts  2.57 us

profile of v3, /device:TPU:0, one launch (start us, length us, event | category | flops | bytes accessed | tf_op | source)
XLA Modules:
  0.0 108.6 jit_solution(15526701255997284555)
XLA Ops:
  0.0 106.1 %shard_map.55 = bf16[800,800]{1,0:T(8,128)(2,1)} custom-call(bf16[800,800]{1,0:T(8,128)(2,1)} %dens.1, s32[8,8]{1,0:T(8,128)} %dmask.1, s32[8,8]{1,0:T(8,128)} %smask.1, s32[8,8]{1,0:T(8,128)} %rmask.1, s32[32]{0:T(128)} %perm.1), custom_call_target="tpu_custom_call" | custom-call | flops 4096000000 | bytes 2560000 | tf_op jit(solution)/shard_map/pallas_call | solution.py:309
  106.1 2.6 %copy.7 = bf16[800,800]{1,0:T(8,128)(2,1)} copy(bf16[800,800]{1,0:T(8,128)(2,1)} %shard_map.55) | data formatting | bytes 2560000

commit v4 on v3

--- a/solution.py
+++ b/solution.py
@@ -11,12 +11,11 @@
 LANES = 128
 
 
-CHUNKS = 3
+CHUNKS = 5
 
 
 def row_chunks(rows):
-    groups = rows // 16
-    sizes = [16 * (groups // CHUNKS + (j < groups % CHUNKS)) for j in range(CHUNKS)]
+    sizes = [rows - 64 * (CHUNKS - 1)] + [64] * (CHUNKS - 1)
     return tuple((sum(sizes[:j]), sizes[j]) for j in range(CHUNKS))
 
 

time: 109 us -> 110 us (level)
  no operation moved by 1% of the time
where the time goes in v4:
time: 110 us; the launch traced here: 109 us
  Pallas kernels  107 us (97%)
  local copies, waits for them, and re-layouts  2.57 us (2%)
    pallas_call x1, Pallas kernels, per_device(): pl.pallas_call(functools.partial(kernel, n, layers), out_shape=jax.ShapeD...  107 us
    unnamed x1, local copies, waits for them, and re-layouts  2.57 us

profile of v4, /device:TPU:0, one launch (start us, length us, event | category | flops | bytes accessed | tf_op | source)
XLA Modules:
  0.0 109.5 jit_solution(3517460028299332245)
XLA Ops:
  0.0 106.9 %shard_map.55 = bf16[800,800]{1,0:T(8,128)(2,1)} custom-call(bf16[800,800]{1,0:T(8,128)(2,1)} %dens.1, s32[8,8]{1,0:T(8,128)} %dmask.1, s32[8,8]{1,0:T(8,128)} %smask.1, s32[8,8]{1,0:T(8,128)} %rmask.1, s32[32]{0:T(128)} %perm.1), custom_call_target="tpu_custom_call" | custom-call | flops 4096000000 | bytes 2560000 | tf_op jit(solution)/shard_map/pallas_call | solution.py:308
  106.9 2.6 %copy.7 = bf16[800,800]{1,0:T(8,128)(2,1)} copy(bf16[800,800]{1,0:T(8,128)(2,1)} %shard_map.55) | data formatting | bytes 2560000
